TPU v7x, 512 devices: a whole 4x8x8 slice. The times are simulated.
512 devices in a mesh: dp: 32 (over x, z), hid: 16 (over y, core).
Axes of the slice: x: 4, y: 8, z: 8, core: 2. Of those that a mesh axis runs over, the one named last changes fastest.
Arguments:
- inputs: bfloat16 [8192, 8192], P('dp', 'hid'), may hold values from -6 to 6
- out_grad: bfloat16 [8192, 8192], P('dp', 'hid'), may hold values from -6 to 6
- home_block: int32 [64], P('hid'), may hold values from 0 to 1
- blocks_up: bfloat16 [64, 3, 256, 256], P('hid', None, 'dp'), may hold values from -0.21875 to 0.21875
- blocks_down: bfloat16 [64, 3, 256, 256], P('hid', None, 'dp'), may hold values from -0.15625 to 0.15625
- up_left: bfloat16 [8192, 128], P('hid', 'dp'), may hold values from -0.0625 to 0.0625
- up_right: bfloat16 [128, 16384], P('dp', 'hid'), may hold values from -0.5 to 0.5
- down_left: bfloat16 [16384, 128], P('hid', 'dp'), may hold values from -0.046875 to 0.046875
- down_right: bfloat16 [128, 8192], P('dp', 'hid'), may hold values from -0.5 to 0.5
Outputs:
- outputs: bfloat16 [8192, 8192], P('dp', 'hid')
- input_grad: bfloat16 [8192, 8192], P('dp', 'hid')
- grad_blocks_up: bfloat16 [64, 3, 256, 256], P('hid', None, 'dp')
- grad_blocks_down: bfloat16 [64, 3, 256, 256], P('hid', None, 'dp')
- grad_up_left: bfloat16 [8192, 128], P('hid', 'dp')
- grad_up_right: bfloat16 [128, 16384], P('dp', 'hid')
- grad_down_left: bfloat16 [16384, 128], P('hid', 'dp')
- grad_down_right: bfloat16 [128, 8192], P('dp', 'hid')
All inputs are finite; a program needn't handle non-finite values.
Results may differ from a plain program's by a relative error of at most 0.022.
Values may be sent and summed in bfloat16 or wider, within the bound.
A program may use at most 64 MiB of HBM per device.

v0:
```python
import jax
import jax.numpy as jnp
from jax import lax
from jax.sharding import PartitionSpec as P

gelu_coef = 0.7978845608028654
cubic_coef = 0.044715


def from_partner(value, axis, distance):
    mask = 2**distance
    pairs = [(source, source ^ mask) for source in range(lax.axis_size(axis))]
    return lax.ppermute(value, axis, pairs)


def gelu_pair(pre_act):
    tangent = jnp.tanh(gelu_coef * (pre_act + cubic_coef * pre_act * pre_act * pre_act))
    activated = 0.5 * pre_act * (1.0 + tangent)
    derivative = 0.5 * (1.0 + tangent) + 0.5 * pre_act * (1.0 - tangent * tangent) * gelu_coef * (
        1.0 + 3.0 * cubic_coef * pre_act * pre_act
    )
    return (activated, derivative)


def per_device(
    inputs, out_grad, home_block, blocks_up, blocks_down, up_left, up_right, down_left, down_right
):
    single = jnp.float32
    half_type = jnp.bfloat16
    highest = lax.Precision.HIGHEST
    row_count, width_dev = inputs.shape
    hid_blocks, slot_count, shard_rows, blk_size = blocks_up.shape
    level_count = slot_count - 1
    in_blocks = width_dev // blk_size
    hidden_dev = hid_blocks * blk_size
    top_bit = lax.axis_size("hid").bit_length() - 1
    grad_scale = float(lax.axis_size("dp") * row_count) ** (-0.5)
    select = (home_block[:, None] == jnp.arange(in_blocks, dtype=jnp.int32)[None, :]).astype(single)
    full_up, full_down, left_in, right_in, left_out, right_out = (
        lax.all_gather(blocks_up, "dp", axis=2, tiled=True),
        lax.all_gather(blocks_down, "dp", axis=2, tiled=True),
        lax.all_gather(up_left, "dp", axis=1, tiled=True),
        lax.all_gather(up_right, "dp", axis=0, tiled=True),
        lax.all_gather(down_left, "dp", axis=1, tiled=True),
        lax.all_gather(down_right, "dp", axis=0, tiled=True),
    )
    rank_in = lax.psum(jnp.dot(inputs, left_in, preferred_element_type=single), "hid")
    rank_in = rank_in.astype(half_type)
    in_pieces = [inputs]
    grad_pieces = [out_grad]
    for level_idx in range(level_count):
        in_pieces.append(from_partner(inputs, "hid", top_bit - 1 - level_idx))

    def pick_blocks(pieces):
        stacked = jnp.stack(pieces, 0).reshape(slot_count, row_count, in_blocks, blk_size)
        return jnp.take(stacked, home_block, axis=2)

    picked = pick_blocks(in_pieces)
    part_rows = picked
    up_sum = jnp.einsum("sthk,hskn->thn", part_rows, full_up, preferred_element_type=single)
    pre_act = up_sum.reshape(row_count, hidden_dev) + jnp.dot(
        rank_in, right_in, preferred_element_type=single
    )
    activated, derivative = gelu_pair(pre_act)
    hidden = activated.astype(half_type)
    hidden_blocks = hidden.reshape(row_count, hid_blocks, blk_size)
    rank_mid = lax.psum(jnp.dot(hidden, left_out, preferred_element_type=single), "hid").astype(
        half_type
    )
    part_rows = hidden_blocks
    down_sum = jnp.einsum("thk,hskn->sthn", part_rows, full_down, preferred_element_type=single)
    placed = jnp.einsum("sthn,hi->stin", down_sum, select, precision=highest)
    total = placed[0]
    for level_idx in range(level_count):
        arrived = from_partner(placed[level_idx + 1], "hid", top_bit - 1 - level_idx)
        total = total + arrived
    outputs = (
        total.reshape(row_count, width_dev)
        + jnp.dot(rank_mid, right_out, preferred_element_type=single)
    ).astype(half_type)
    rank_back = lax.psum(jnp.dot(out_grad, right_out.T, preferred_element_type=single), "hid")
    rank_back = rank_back.astype(half_type)
    for level_idx in range(level_count):
        grad_pieces.append(from_partner(out_grad, "hid", top_bit - 1 - level_idx))
    grad_picked = pick_blocks(grad_pieces)
    grad_hidden = jnp.einsum(
        "sthn,hskn->thk", grad_picked, full_down, preferred_element_type=single
    )
    grad_pre = (
        (
            grad_hidden.reshape(row_count, hidden_dev)
            + jnp.dot(rank_back, left_out.T, preferred_element_type=single)
        )
        * derivative
    ).astype(half_type)
    rank_grad = lax.psum(
        jnp.dot(grad_pre, right_in.T, preferred_element_type=single), "hid"
    ).astype(half_type)
    grad_blocks = grad_pre.reshape(row_count, hid_blocks, blk_size)
    back_sum = jnp.einsum("thn,hskn->sthk", grad_blocks, full_up, preferred_element_type=single)
    back_placed = jnp.einsum("sthk,hi->stik", back_sum, select, precision=highest)
    back_total = back_placed[0]
    for level_idx in range(level_count):
        arrived = from_partner(back_placed[level_idx + 1], "hid", top_bit - 1 - level_idx)
        back_total = back_total + arrived
    input_grad = (
        back_total.reshape(row_count, width_dev)
        + jnp.dot(rank_grad, left_in.T, preferred_element_type=single)
    ).astype(half_type)
    summed = (
        lax.psum_scatter(
            (
                grad_scale
                * jnp.einsum("sthk,thn->hskn", picked, grad_blocks, preferred_element_type=single)
            ).astype(jnp.bfloat16),
            "dp",
            scatter_dimension=2,
            tiled=True,
        ).astype(jnp.float32),
        lax.psum_scatter(
            (
                grad_scale
                * jnp.einsum(
                    "thk,sthn->hskn", hidden_blocks, grad_picked, preferred_element_type=single
                )
            ).astype(jnp.bfloat16),
            "dp",
            scatter_dimension=2,
            tiled=True,
        ).astype(jnp.float32),
        lax.psum_scatter(
            (grad_scale * jnp.dot(inputs.T, rank_grad, preferred_element_type=single)).astype(
                jnp.bfloat16
            ),
            "dp",
            scatter_dimension=1,
            tiled=True,
        ).astype(jnp.float32),
        lax.psum_scatter(
            (grad_scale * jnp.dot(rank_in.T, grad_pre, preferred_element_type=single)).astype(
                jnp.bfloat16
            ),
            "dp",
            scatter_dimension=0,
            tiled=True,
        ).astype(jnp.float32),
        lax.psum_scatter(
            (grad_scale * jnp.dot(hidden.T, rank_back, preferred_element_type=single)).astype(
                jnp.bfloat16
            ),
            "dp",
            scatter_dimension=1,
            tiled=True,
        ).astype(jnp.float32),
        lax.psum_scatter(
            (grad_scale * jnp.dot(rank_mid.T, out_grad, preferred_element_type=single)).astype(
                jnp.bfloat16
            ),
            "dp",
            scatter_dimension=0,
            tiled=True,
        ).astype(jnp.float32),
    )
    return (outputs, input_grad) + tuple((summed_part.astype(half_type) for summed_part in summed))


def solution(mesh):
    placed = (
        P("dp", "hid"),
        P("dp", "hid"),
        P("hid"),
        P("hid", None, "dp", None),
        P("hid", None, "dp", None),
        P("hid", "dp"),
        P("dp", "hid"),
        P("hid", "dp"),
        P("dp", "hid"),
    )
    return jax.shard_map(
        per_device,
        mesh=mesh,
        in_specs=placed,
        out_specs=(
            P("dp", "hid"),
            P("dp", "hid"),
            P("hid", None, "dp", None),
            P("hid", None, "dp", None),
            P("hid", "dp"),
            P("dp", "hid"),
            P("hid", "dp"),
            P("dp", "hid"),
        ),
        check_vma=False,
    )
```

profile of v0, /device:TPU:8, one launch (start us, length us, event | category | flops | bytes accessed | tf_op | source)
XLA Modules:
  0.0 738.6 jit_solution(1994460682840392459)
XLA Ops:
  9.8 6.8 collective-permute-start
  16.7 2.7 collective-permute-start.1
  20.5 4.7 collective-permute-start.4
  25.2 2.2 collective-permute-start.5
  27.6 49.3 %all-gather = bf16[32,4,512]{2,1,0:T(4,128)(2,1)S(1)} all-gather(bf16[1,4,512]{2,1,0:T(4,128)(2,1)S(1)} %bitcast.138), channel_id=1, replica_groups=mesh['dp'=32,'hid'=16] {'dp'}, dimensions={0}, use_global_device_ids=true | all-gather | bytes 135168 | tf_op jit(solution)/shard_map/all_gather | solution.py:42
  77.2 42.4 %all-gather.3 = bf16[32,4,512]{2,1,0:T(4,128)(2,1)S(1)} all-gather(bf16[1,4,512]{2,1,0:T(4,128)(2,1)S(1)} %bitcast.139), channel_id=1, replica_groups=mesh['dp'=32,'hid'=16] {'dp'}, dimensions={0}, use_global_device_ids=true | all-gather | bytes 135168 | tf_op jit(solution)/shard_map/all_gather | solution.py:45
  119.9 46.7 %all-gather.1 = bf16[32,4,1024]{2,1,0:T(4,128)(2,1)S(1)} all-gather(bf16[1,4,1024]{2,1,0:T(4,128)(2,1)S(1)} %bitcast.136), channel_id=1, replica_groups=mesh['dp'=32,'hid'=16] {'dp'}, dimensions={0}, use_global_device_ids=true | all-gather | bytes 270336 | tf_op jit(solution)/shard_map/all_gather | solution.py:43
  167.6 45.5 %all-reduce.13 = (bf16[256,128]{1,0:T(8,128)(2,1)S(1)}, bf16[256,128]{1,0:T(8,128)(2,1)S(1)}) all-reduce(f32[256,128]{1,0:T(8,128)S(1)} %fusion.57, f32[256,128]{1,0:T(8,128)S(1)} %fusion.59), channel_id=1, replica_groups=mesh['dp'=32,'hid'=16] {'hid'}, use_global_device_ids=true, to_apply=%region_0.2 | all-reduce | flops 65536 | bytes 393216 | tf_op jit(solution)/shard_map/psum | solution.py:47
  213.1 48.1 %all-gather.2 = bf16[32,4,1024]{2,1,0:T(4,128)(2,1)S(1)} all-gather(bf16[1,4,1024]{2,1,0:T(4,128)(2,1)S(1)} %bitcast.137), channel_id=1, replica_groups=mesh['dp'=32,'hid'=16] {'dp'}, dimensions={0}, use_global_device_ids=true | all-gather | bytes 270336 | tf_op jit(solution)/shard_map/all_gather | solution.py:44
  264.7 1.8 pad_maximum_fusion.1
  266.5 1.9 gather_fusion.1
  268.4 3.2 fusion.8
  271.6 2.6 copy.60
  274.2 3.1 fusion.5
  277.4 2.7 copy.89
  285.1 48.0 %all-reduce.14 = (bf16[256,128]{1,0:T(8,128)(2,1)S(1)}, bf16[256,128]{1,0:T(8,128)(2,1)S(1)}) all-reduce(f32[256,128]{1,0:T(8,128)S(1)} %fusion.58, f32[256,128]{1,0:T(8,128)S(1)} %fusion.60), channel_id=1, replica_groups=mesh['dp'=32,'hid'=16] {'hid'}, use_global_device_ids=true, to_apply=%region_1.0 | all-reduce | flops 65536 | bytes 393216 | tf_op jit(solution)/shard_map/psum | solution.py:67
  334.8 2.3 fusion.10
  337.1 2.4 copy.76
  339.7 1.4 dynamic-slice
  343.7 1.4 copy.117
  345.0 2.9 reshape.97
  347.9 1.4 copy-done.3
  349.9 4.1 fusion.16
  354.4 7.7 %collective-permute-start.6 = (f32[256,2,256]{2,1,0:T(2,128)S(1)}, f32[256,2,256]{2,1,0:T(2,128)S(1)}, u32[]{:S(2)}, u32[]{:S(2)}) collective-permute-start(f32[256,2,256]{2,1,0:T(2,128)S(1)} %get-tuple-element.50), channel_id=1, source_target_pairs={{0,8},{1,9},{2,10},{3,11},{4,12},{5,13},{6,14},{7,15},{8,0},{9,1},... | collective-permute-start | bytes 1572872 | tf_op jit(solution)/shard_map/ppermute | solution.py:13
  362.1 1.9 collective-permute-start.7
  364.6 4.1 fusion.13
  369.1 7.0 collective-permute-start.2
  376.1 1.9 collective-permute-start.3
  378.4 62.6 %collective-permute-done.7 = f32[256,2,256]{2,1,0:T(2,128)S(1)} collective-permute-done((f32[256,2,256]{2,1,0:T(2,128)S(1)}, f32[256,2,256]{2,1,0:T(2,128)S(1)}, u32[]{:S(2)}, u32[]{:S(2)}) %collective-permute-start.7) | collective-permute-done | bytes 524320 | tf_op jit(solution)/shard_map/ppermute | solution.py:13
  441.4 10.7 %collective-permute-done.3 = f32[256,2,256]{2,1,0:T(2,128)S(1)} collective-permute-done((f32[256,2,256]{2,1,0:T(2,128)S(1)}, f32[256,2,256]{2,1,0:T(2,128)S(1)}, u32[]{:S(2)}, u32[]{:S(2)}) %collective-permute-start.3) | collective-permute-done | bytes 524320 | tf_op jit(solution)/shard_map/ppermute | solution.py:13
  453.5 52.5 %all-reduce.12.cloned.1.call-done = (bf16[4,3,256,256]{3,0,1,2:T(4,128)(2,1)}, bf16[512,128]{0,1:T(8,128)(2,1)}, bf16[128,1024]{1,0:T(8,128)(2,1)}, bf16[1024,128]{0,1:T(8,128)(2,1)}, bf16[128,512]{1,0:T(8,128)(2,1)}) async-done(((bf16[4,3,256,256]{3,0,1,2:T(4,128)(2,1)}, bf16[512,128]{0,1:T(8,128)(2,1)}, bf16[128,1024]{1,0:T(8,128)(2,1)}, bf16[1024,128]{0,1:T(8,128)(2,1)}, bf16[128,512]{1,0:T(8,128)(2,1)}), ...) | async-done | bytes 2359312
  512.6 218.0 %reduce-scatter.4.cloned.1.call-done = bf16[8,3072]{1,0:T(8,128)(2,1)} async-done(((bf16[256,3072]{1,0:T(8,128)(2,1)}), bf16[8,3072]{1,0:T(8,128)(2,1)}) %reduce-scatter.4.cloned.1.call-update) | async-done | bytes 49168
  (94 shorter events, 29.2 us)
Async XLA Ops:
  7.2 69.8 %copy-start.2 = (bf16[256,512]{1,0:T(8,128)(2,1)S(1)}, bf16[256,512]{1,0:T(8,128)(2,1)}, u32[]{:S(2)}) copy-start(bf16[256,512]{1,0:T(8,128)(2,1)} %param.11) | copy-start | bytes 786436
  7.2 112.5 %copy-start.1 = (bf16[256,512]{1,0:T(8,128)(2,1)S(1)}, bf16[256,512]{1,0:T(8,128)(2,1)}, u32[]{:S(2)}) copy-start(bf16[256,512]{1,0:T(8,128)(2,1)} %param.12) | copy-start | bytes 786436
  7.2 20.4 %copy-start.12 = (bf16[512,4]{0,1:T(4,128)(2,1)S(1)}, bf16[512,4]{0,1:T(4,128)(2,1)}, u32[]{:S(2)}) copy-start(bf16[512,4]{0,1:T(4,128)(2,1)} %param.16) | copy-start | bytes 12292
  7.2 70.0 %copy-start.13 = (bf16[4,512]{1,0:T(4,128)(2,1)S(1)}, bf16[4,512]{1,0:T(4,128)(2,1)}, u32[]{:S(2)}) copy-start(bf16[4,512]{1,0:T(4,128)(2,1)} %param.19) | copy-start | bytes 12292
  7.2 261.2 %all-gather.7.cloned.1.call-start = ((), (), s32[]{:S(2)}) async-start(), calls=%async_computation.1 | async-start | bytes 1622016 | tf_op jit(solution)/shard_map/all_gather | solution.py:40
  7.9 266.3 %all-gather.9.cloned.1.call-start = ((), (), s32[]{:S(2)}) async-start(), calls=%async_computation.2 | async-start | bytes 1622016 | tf_op jit(solution)/shard_map/all_gather | solution.py:41
  8.7 497.2 %all-reduce.12.cloned.1.call-start = ((), (), s32[]{:S(2)}) async-start(), calls=%async_computation.4 | async-start | bytes 4718592
  9.8 110.1 %copy-start.10 = (bf16[4,1024]{1,0:T(4,128)(2,1)S(1)}, bf16[4,1024]{1,0:T(4,128)(2,1)}, u32[]{:S(2)}) copy-start(bf16[4,1024]{1,0:T(4,128)(2,1)} %param.17) | copy-start | bytes 24580
  9.8 252.2 %collective-permute-start = (bf16[256,512]{0,1:T(8,128)(2,1)S(1)}, bf16[256,512]{0,1:T(8,128)(2,1)S(1)}, u32[]{:S(2)}, u32[]{:S(2)}) collective-permute-start(bf16[256,512]{0,1:T(8,128)(2,1)S(1)} %copy.54), channel_id=1, source_target_pairs={{0,8},{1,9},{2,10},{3,11},{4,12},{5,13},{6,14},{7,15},{8,0},{9,1},... | collective-permute-start | bytes 786440 | tf_op jit(solution)/shard_map/ppermute | solution.py:13
  16.7 245.5 %collective-permute-start.1 = (bf16[256,512]{0,1:T(8,128)(2,1)S(1)}, bf16[256,512]{0,1:T(8,128)(2,1)S(1)}, u32[]{:S(2)}, u32[]{:S(2)}) collective-permute-start(bf16[256,512]{0,1:T(8,128)(2,1)S(1)} %copy.54), channel_id=1, source_target_pairs={{0,4},{1,5},{2,6},{3,7},{4,0},{5,1},{6,2},{7,3},{8,12},{9,13},{10,... | collective-permute-start | bytes 786440 | tf_op jit(solution)/shard_map/ppermute | solution.py:13
  20.5 241.8 %collective-permute-start.4 = (bf16[256,512]{0,1:T(8,128)(2,1)S(1)}, bf16[256,512]{0,1:T(8,128)(2,1)S(1)}, u32[]{:S(2)}, u32[]{:S(2)}) collective-permute-start(bf16[256,512]{0,1:T(8,128)(2,1)S(1)} %copy.63), channel_id=1, source_target_pairs={{0,8},{1,9},{2,10},{3,11},{4,12},{5,13},{6,14},{7,15},{8,0},{9,1},... | collective-permute-start | bytes 786440 | tf_op jit(solution)/shard_map/ppermute | solution.py:13
  25.2 237.9 %collective-permute-start.5 = (bf16[256,512]{0,1:T(8,128)(2,1)S(1)}, bf16[256,512]{0,1:T(8,128)(2,1)S(1)}, u32[]{:S(2)}, u32[]{:S(2)}) collective-permute-start(bf16[256,512]{0,1:T(8,128)(2,1)S(1)} %copy.63), channel_id=1, source_target_pairs={{0,4},{1,5},{2,6},{3,7},{4,0},{5,1},{6,2},{7,3},{8,12},{9,13},{10,... | collective-permute-start | bytes 786440 | tf_op jit(solution)/shard_map/ppermute | solution.py:13
  27.6 139.9 %copy-start.14 = (s32[4]{0:T(128)S(1)}, s32[4]{0:T(128)}, u32[]{:S(2)}) copy-start(s32[4]{0:T(128)} %param.13) | copy-start | bytes 52
  77.0 136.1 %copy-start.11 = (bf16[1024,4]{0,1:T(4,128)(2,1)S(1)}, bf16[1024,4]{0,1:T(4,128)(2,1)}, u32[]{:S(2)}) copy-start(bf16[1024,4]{0,1:T(4,128)(2,1)} %param.18) | copy-start | bytes 24580
  264.7 3.6 copy-start.4
  271.6 2.7 copy-start.6
  277.4 2.7 copy-start.8
  280.1 0.9 copy-start.7
  280.1 1.3 copy-start.9
  339.5 3.3 copy-start.5
  339.5 391.1 %reduce-scatter.4.cloned.1.call-start = ((), (), s32[]{:S(2)}) async-start(), calls=%async_computation.3 | async-start | bytes 1622016
  347.9 1.4 copy-start.3
  354.0 10.0 %copy-start = (bf16[4,3,256,256]{3,2,1,0:T(8,128)(2,1)S(1)}, bf16[4,3,256,256]{3,2,1,0:T(8,128)(2,1)}, u32[]{:S(2)}) copy-start(bf16[4,3,256,256]{3,2,1,0:T(8,128)(2,1)} %all-gather.9.cloned.1.call-done) | copy-start | bytes 4718596
  354.4 24.0 %collective-permute-start.6 = (f32[256,2,256]{2,1,0:T(2,128)S(1)}, f32[256,2,256]{2,1,0:T(2,128)S(1)}, u32[]{:S(2)}, u32[]{:S(2)}) collective-permute-start(f32[256,2,256]{2,1,0:T(2,128)S(1)} %get-tuple-element.50), channel_id=1, source_target_pairs={{0,8},{1,9},{2,10},{3,11},{4,12},{5,13},{6,14},{7,15},{8,0},{9,1},... | collective-permute-start | bytes 1572872 | tf_op jit(solution)/shard_map/ppermute | solution.py:13
  362.1 78.9 %collective-permute-start.7 = (f32[256,2,256]{2,1,0:T(2,128)S(1)}, f32[256,2,256]{2,1,0:T(2,128)S(1)}, u32[]{:S(2)}, u32[]{:S(2)}) collective-permute-start(f32[256,2,256]{2,1,0:T(2,128)S(1)} %get-tuple-element.51), channel_id=1, source_target_pairs={{0,4},{1,5},{2,6},{3,7},{4,0},{5,1},{6,2},{7,3},{8,12},{9,13},{10,... | collective-permute-start | bytes 1572872 | tf_op jit(solution)/shard_map/ppermute | solution.py:13
  369.1 72.3 %collective-permute-start.2 = (f32[256,2,256]{2,1,0:T(2,128)S(1)}, f32[256,2,256]{2,1,0:T(2,128)S(1)}, u32[]{:S(2)}, u32[]{:S(2)}) collective-permute-start(f32[256,2,256]{2,1,0:T(2,128)S(1)} %get-tuple-element.52), channel_id=1, source_target_pairs={{0,8},{1,9},{2,10},{3,11},{4,12},{5,13},{6,14},{7,15},{8,0},{9,1},... | collective-permute-start | bytes 1572872 | tf_op jit(solution)/shard_map/ppermute | solution.py:13
  376.1 76.1 %collective-permute-start.3 = (f32[256,2,256]{2,1,0:T(2,128)S(1)}, f32[256,2,256]{2,1,0:T(2,128)S(1)}, u32[]{:S(2)}, u32[]{:S(2)}) collective-permute-start(f32[256,2,256]{2,1,0:T(2,128)S(1)} %get-tuple-element.53), channel_id=1, source_target_pairs={{0,4},{1,5},{2,6},{3,7},{4,0},{5,1},{6,2},{7,3},{8,12},{9,13},{10,... | collective-permute-start | bytes 1572872 | tf_op jit(solution)/shard_map/ppermute | solution.py:13
Sparse Core Ops, SparseCore 0:
  11.1 83.7 all-gather.6
  97.9 77.6 all-gather.8
  339.6 166.2 all-reduce.11
  510.8 219.7 reduce-scatter.3
where the time goes:
time: 740 us; the launch traced here: 739 us
  waiting for transfers between devices  345 us (47%)
  blocking collectives  280 us (38%)
  starting transfers between devices  35.3 us (5%)
  local copies, waits for them, and re-layouts  33.8 us (5%)
  matrix products  25.2 us (3%)
  between operations  15.6 us (2%)
    unnamed x6, waiting for transfers between devices  272 us
    ppermute x8, waiting for transfers between devices, from_partner(): return lax.ppermute(value, axis, pairs)  73.3 us
    all_gather x1, blocking collectives, per_device(): lax.all_gather(up_left, 'dp', axis=1, tiled=True)  49.3 us
    all_gather x1, blocking collectives, per_device(): lax.all_gather(down_left, 'dp', axis=1, tiled=True)  48.1 us
    psum x1, blocking collectives, per_device(): lax.psum(jnp.dot(hidden, left_out, preferred_element_type=single), 'hid')  48 us
    all_gather x1, blocking collectives, per_device(): lax.all_gather(up_right, 'dp', axis=0, tiled=True)  46.7 us
    psum x1, blocking collectives, per_device(): lax.psum(jnp.dot(inputs, left_in, preferred_element_type=single), 'hid')  45.5 us
    all_gather x1, blocking collectives, per_device(): lax.all_gather(down_right, 'dp', axis=0, tiled=True)  42.4 us
  transfers between devices with their start and end apart: 12, of which 4 were waited for; matrix products, arithmetic and copies ran while one was open for 6% of the time, Pallas kernels for 0%

commit v1 on v0

--- a/solution.py
+++ b/solution.py
@@ -40,7 +40,9 @@
         lax.all_gather(blocks_up, "dp", axis=2, tiled=True),
         lax.all_gather(blocks_down, "dp", axis=2, tiled=True),
         lax.all_gather(up_left, "dp", axis=1, tiled=True),
-        lax.all_gather(up_right, "dp", axis=0, tiled=True),
+        jnp.concatenate(
+            lax.all_to_all(jnp.stack([up_right] * lax.axis_size("dp")), "dp", 0, 0), axis=0
+        ),
         lax.all_gather(down_left, "dp", axis=1, tiled=True),
         lax.all_gather(down_right, "dp", axis=0, tiled=True),
     )

time: 740 us -> 704 us (0.951)
  blocking collectives: 280 us -> 228 us
  starting transfers between devices: 35.3 us -> 48.3 us
    all_gather x1 -> x0, blocking collectives: 46.7 us -> none  [per_device(): lax.all_gather(up_right, 'dp', axis=0, tiled=True)]
    all_to_all x0 -> x1, starting transfers between devices: none -> 13.3 us  [per_device(): lax.all_to_all(jnp.stack([up_right] * lax.axis_size('dp')), 'dp', 0, 0)]
    unnamed x49 -> x44, local copies, waits for them, and re-layouts: 19.2 us -> 18.4 us
  transfers between devices with their start and end apart: 12 -> 13, of which waited for: 4 -> 4; matrix products, arithmetic and copies ran while one was open for 6% -> 6% of each run, Pallas kernels for 0% -> 0%
where the time goes in v1:
time: 704 us; the launch traced here: 703 us
  waiting for transfers between devices  348 us (49%)
  blocking collectives  228 us (32%)
  starting transfers between devices  48.3 us (7%)
  local copies, waits for them, and re-layouts  35.5 us (5%)
  matrix products  25.2 us (4%)
  between operations  15.6 us (2%)
    unnamed x6, waiting for transfers between devices  274 us
    ppermute x8, waiting for transfers between devices, from_partner(): return lax.ppermute(value, axis, pairs)  73.2 us
    psum x1, blocking collectives, per_device(): lax.psum(jnp.dot(hidden, left_out, preferred_element_type=single), 'hid')  47.9 us
    all_gather x1, blocking collectives, per_device(): lax.all_gather(down_left, 'dp', axis=1, tiled=True)  47.8 us
    psum x1, blocking collectives, per_device(): lax.psum(jnp.dot(inputs, left_in, preferred_element_type=single), 'hid')  46.1 us
    all_gather x1, blocking collectives, per_device(): lax.all_gather(up_left, 'dp', axis=1, tiled=True)  43.9 us
    all_gather x1, blocking collectives, per_device(): lax.all_gather(down_right, 'dp', axis=0, tiled=True)  41.8 us
    ppermute x8, starting transfers between devices, from_partner(): return lax.ppermute(value, axis, pairs)  34.7 us
  transfers between devices with their start and end apart: 13, of which 4 were waited for; matrix products, arithmetic and copies ran while one was open for 6% of the time, Pallas kernels for 0%

profile of v1, /device:TPU:8, one launch (start us, length us, event | category | flops | bytes accessed | tf_op | source)
XLA Modules:
  0.0 703.2 jit_solution(16605383848177542700)
XLA Ops:
  9.8 6.8 collective-permute-start
  16.7 2.7 collective-permute-start.1
  20.5 4.7 collective-permute-start.4
  25.2 2.2 collective-permute-start.5
  27.5 1.5 stack.22
  28.9 13.3 %all-to-all-start = ((bf16[32,4,1024]{2,1,0:T(4,128)(2,1)}), bf16[32,4,1024]{2,1,0:T(4,128)(2,1)}, u32[]{:S(2)}, u32[]{:S(2)}) async-start(bf16[32,4,1024]{2,1,0:T(4,128)(2,1)} %stack.22), calls=%async_computation | async-start | bytes 524288 | tf_op jit(solution)/shard_map/all_to_all | solution.py:44
  42.3 43.9 %all-gather = bf16[32,4,512]{2,1,0:T(4,128)(2,1)S(1)} all-gather(bf16[1,4,512]{2,1,0:T(4,128)(2,1)S(1)} %bitcast.136), channel_id=1, replica_groups=mesh['dp'=32,'hid'=16] {'dp'}, dimensions={0}, use_global_device_ids=true | all-gather | bytes 135168 | tf_op jit(solution)/shard_map/all_gather | solution.py:42
  86.5 41.8 %all-gather.2 = bf16[32,4,512]{2,1,0:T(4,128)(2,1)S(1)} all-gather(bf16[1,4,512]{2,1,0:T(4,128)(2,1)S(1)} %bitcast.137), channel_id=1, replica_groups=mesh['dp'=32,'hid'=16] {'dp'}, dimensions={0}, use_global_device_ids=true | all-gather | bytes 135168 | tf_op jit(solution)/shard_map/all_gather | solution.py:47
  128.6 46.1 %all-reduce.13 = (bf16[256,128]{1,0:T(8,128)(2,1)S(1)}, bf16[256,128]{1,0:T(8,128)(2,1)S(1)}) all-reduce(f32[256,128]{1,0:T(8,128)S(1)} %fusion.57, f32[256,128]{1,0:T(8,128)S(1)} %fusion.59), channel_id=1, replica_groups=mesh['dp'=32,'hid'=16] {'hid'}, use_global_device_ids=true, to_apply=%region_0.2 | all-reduce | flops 65536 | bytes 393216 | tf_op jit(solution)/shard_map/psum | solution.py:49
  174.7 47.8 %all-gather.1 = bf16[32,4,1024]{2,1,0:T(4,128)(2,1)S(1)} all-gather(bf16[1,4,1024]{2,1,0:T(4,128)(2,1)S(1)} %bitcast.135), channel_id=1, replica_groups=mesh['dp'=32,'hid'=16] {'dp'}, dimensions={0}, use_global_device_ids=true | all-gather | bytes 270336 | tf_op jit(solution)/shard_map/all_gather | solution.py:46
  226.4 1.8 pad_maximum_fusion.1
  228.2 1.9 gather_fusion.1
  231.1 3.2 fusion.8
  234.3 2.6 copy.60
  236.9 3.1 fusion.5
  240.1 2.7 copy.89
  247.7 47.9 %all-reduce.14 = (bf16[256,128]{1,0:T(8,128)(2,1)S(1)}, bf16[256,128]{1,0:T(8,128)(2,1)S(1)}) all-reduce(f32[256,128]{1,0:T(8,128)S(1)} %fusion.58, f32[256,128]{1,0:T(8,128)S(1)} %fusion.60), channel_id=1, replica_groups=mesh['dp'=32,'hid'=16] {'hid'}, use_global_device_ids=true, to_apply=%region_1.0 | all-reduce | flops 65536 | bytes 393216 | tf_op jit(solution)/shard_map/psum | solution.py:69
  297.4 2.3 fusion.10
  299.7 2.4 copy.76
  302.3 1.4 dynamic-slice
  307.6 2.9 reshape.101
  310.5 1.4 copy-done.3
  312.5 4.1 fusion.16
  317.0 7.3 %collective-permute-start.6 = (f32[256,2,256]{2,1,0:T(2,128)S(1)}, f32[256,2,256]{2,1,0:T(2,128)S(1)}, u32[]{:S(2)}, u32[]{:S(2)}) collective-permute-start(f32[256,2,256]{2,1,0:T(2,128)S(1)} %get-tuple-element.50), channel_id=1, source_target_pairs={{0,8},{1,9},{2,10},{3,11},{4,12},{5,13},{6,14},{7,15},{8,0},{9,1},... | collective-permute-start | bytes 1572872 | tf_op jit(solution)/shard_map/ppermute | solution.py:13
  324.3 1.9 collective-permute-start.7
  326.8 4.1 fusion.13
  331.3 7.0 collective-permute-start.2
  338.3 1.9 collective-permute-start.3
  340.7 62.5 %collective-permute-done.7 = f32[256,2,256]{2,1,0:T(2,128)S(1)} collective-permute-done((f32[256,2,256]{2,1,0:T(2,128)S(1)}, f32[256,2,256]{2,1,0:T(2,128)S(1)}, u32[]{:S(2)}, u32[]{:S(2)}) %collective-permute-start.7) | collective-permute-done | bytes 524320 | tf_op jit(solution)/shard_map/ppermute | solution.py:13
  403.6 10.8 %collective-permute-done.3 = f32[256,2,256]{2,1,0:T(2,128)S(1)} collective-permute-done((f32[256,2,256]{2,1,0:T(2,128)S(1)}, f32[256,2,256]{2,1,0:T(2,128)S(1)}, u32[]{:S(2)}, u32[]{:S(2)}) %collective-permute-start.3) | collective-permute-done | bytes 524320 | tf_op jit(solution)/shard_map/ppermute | solution.py:13
  415.7 54.9 %all-reduce.12.cloned.1.call-done = (bf16[4,3,256,256]{3,0,1,2:T(4,128)(2,1)}, bf16[512,128]{0,1:T(8,128)(2,1)}, bf16[128,1024]{1,0:T(8,128)(2,1)}, bf16[1024,128]{0,1:T(8,128)(2,1)}, bf16[128,512]{1,0:T(8,128)(2,1)}) async-done(((bf16[4,3,256,256]{3,0,1,2:T(4,128)(2,1)}, bf16[512,128]{0,1:T(8,128)(2,1)}, bf16[128,1024]{1,0:T(8,128)(2,1)}, bf16[1024,128]{0,1:T(8,128)(2,1)}, bf16[128,512]{1,0:T(8,128)(2,1)}), ...) | async-done | bytes 2359312
  477.2 218.0 %reduce-scatter.4.cloned.1.call-done = bf16[8,3072]{1,0:T(8,128)(2,1)} async-done(((bf16[256,3072]{1,0:T(8,128)(2,1)}), bf16[8,3072]{1,0:T(8,128)(2,1)}) %reduce-scatter.4.cloned.1.call-update) | async-done | bytes 49168
  (92 shorter events, 30.8 us)
Async XLA Ops:
  7.2 79.1 %copy-start.2 = (bf16[256,512]{1,0:T(8,128)(2,1)S(1)}, bf16[256,512]{1,0:T(8,128)(2,1)}, u32[]{:S(2)}) copy-start(bf16[256,512]{1,0:T(8,128)(2,1)} %param.11) | copy-start | bytes 786436
  7.2 35.1 %copy-start.10 = (bf16[512,4]{0,1:T(4,128)(2,1)S(1)}, bf16[512,4]{0,1:T(4,128)(2,1)}, u32[]{:S(2)}) copy-start(bf16[512,4]{0,1:T(4,128)(2,1)} %param.16) | copy-start | bytes 12292
  7.2 79.3 %copy-start.11 = (bf16[4,512]{1,0:T(4,128)(2,1)S(1)}, bf16[4,512]{1,0:T(4,128)(2,1)}, u32[]{:S(2)}) copy-start(bf16[4,512]{1,0:T(4,128)(2,1)} %param.19) | copy-start | bytes 12292
  7.2 223.9 %all-gather.6.cloned.1.call-start = ((), (), s32[]{:S(2)}) async-start(), calls=%async_computation.2 | async-start | bytes 1622016 | tf_op jit(solution)/shard_map/all_gather | solution.py:40
  7.9 229.0 %all-gather.8.cloned.1.call-start = ((), (), s32[]{:S(2)}) async-start(), calls=%async_computation.3 | async-start | bytes 1622016 | tf_op jit(solution)/shard_map/all_gather | solution.py:41
  8.7 119.7 %copy-start.1 = (bf16[256,512]{1,0:T(8,128)(2,1)S(1)}, bf16[256,512]{1,0:T(8,128)(2,1)}, u32[]{:S(2)}) copy-start(bf16[256,512]{1,0:T(8,128)(2,1)} %param.12) | copy-start | bytes 786436
  9.8 118.8 %copy-start.12 = (s32[4]{0:T(128)S(1)}, s32[4]{0:T(128)}, u32[]{:S(2)}) copy-start(s32[4]{0:T(128)} %param.13) | copy-start | bytes 52
  9.8 213.8 %collective-permute-start = (bf16[256,512]{0,1:T(8,128)(2,1)S(1)}, bf16[256,512]{0,1:T(8,128)(2,1)S(1)}, u32[]{:S(2)}, u32[]{:S(2)}) collective-permute-start(bf16[256,512]{0,1:T(8,128)(2,1)S(1)} %copy.54), channel_id=1, source_target_pairs={{0,8},{1,9},{2,10},{3,11},{4,12},{5,13},{6,14},{7,15},{8,0},{9,1},... | collective-permute-start | bytes 786440 | tf_op jit(solution)/shard_map/ppermute | solution.py:13
  16.7 207.1 %collective-permute-start.1 = (bf16[256,512]{0,1:T(8,128)(2,1)S(1)}, bf16[256,512]{0,1:T(8,128)(2,1)S(1)}, u32[]{:S(2)}, u32[]{:S(2)}) collective-permute-start(bf16[256,512]{0,1:T(8,128)(2,1)S(1)} %copy.54), channel_id=1, source_target_pairs={{0,4},{1,5},{2,6},{3,7},{4,0},{5,1},{6,2},{7,3},{8,12},{9,13},{10,... | collective-permute-start | bytes 786440 | tf_op jit(solution)/shard_map/ppermute | solution.py:13
  20.5 154.3 %copy-start.9 = (bf16[1024,4]{0,1:T(4,128)(2,1)S(1)}, bf16[1024,4]{0,1:T(4,128)(2,1)}, u32[]{:S(2)}) copy-start(bf16[1024,4]{0,1:T(4,128)(2,1)} %param.18) | copy-start | bytes 24580
  20.5 203.4 %collective-permute-start.4 = (bf16[256,512]{0,1:T(8,128)(2,1)S(1)}, bf16[256,512]{0,1:T(8,128)(2,1)S(1)}, u32[]{:S(2)}, u32[]{:S(2)}) collective-permute-start(bf16[256,512]{0,1:T(8,128)(2,1)S(1)} %copy.63), channel_id=1, source_target_pairs={{0,8},{1,9},{2,10},{3,11},{4,12},{5,13},{6,14},{7,15},{8,0},{9,1},... | collective-permute-start | bytes 786440 | tf_op jit(solution)/shard_map/ppermute | solution.py:13
  25.2 199.6 %collective-permute-start.5 = (bf16[256,512]{0,1:T(8,128)(2,1)S(1)}, bf16[256,512]{0,1:T(8,128)(2,1)S(1)}, u32[]{:S(2)}, u32[]{:S(2)}) collective-permute-start(bf16[256,512]{0,1:T(8,128)(2,1)S(1)} %copy.63), channel_id=1, source_target_pairs={{0,4},{1,5},{2,6},{3,7},{4,0},{5,1},{6,2},{7,3},{8,12},{9,13},{10,... | collective-permute-start | bytes 786440 | tf_op jit(solution)/shard_map/ppermute | solution.py:13
  28.9 201.1 %all-to-all-start = ((bf16[32,4,1024]{2,1,0:T(4,128)(2,1)}), bf16[32,4,1024]{2,1,0:T(4,128)(2,1)}, u32[]{:S(2)}, u32[]{:S(2)}) async-start(bf16[32,4,1024]{2,1,0:T(4,128)(2,1)} %stack.22), calls=%async_computation | async-start | bytes 524288 | tf_op jit(solution)/shard_map/all_to_all | solution.py:44
  42.2 428.3 %all-reduce.12.cloned.1.call-start = ((), (), s32[]{:S(2)}) async-start(), calls=%async_computation.5 | async-start | bytes 4718592
  226.4 4.7 copy-start.4
  234.3 2.7 copy-start.6
  240.1 2.7 copy-start.7
  242.8 1.2 copy-start.8
  302.0 3.3 copy-start.5
  302.1 393.1 %reduce-scatter.4.cloned.1.call-start = ((), (), s32[]{:S(2)}) async-start(), calls=%async_computation.4 | async-start | bytes 1622016
  310.5 1.4 copy-start.3
  316.6 9.7 %copy-start = (bf16[4,3,256,256]{3,2,1,0:T(8,128)(2,1)S(1)}, bf16[4,3,256,256]{3,2,1,0:T(8,128)(2,1)}, u32[]{:S(2)}) copy-start(bf16[4,3,256,256]{3,2,1,0:T(8,128)(2,1)} %all-gather.8.cloned.1.call-done) | copy-start | bytes 4718596
  317.0 23.7 %collective-permute-start.6 = (f32[256,2,256]{2,1,0:T(2,128)S(1)}, f32[256,2,256]{2,1,0:T(2,128)S(1)}, u32[]{:S(2)}, u32[]{:S(2)}) collective-permute-start(f32[256,2,256]{2,1,0:T(2,128)S(1)} %get-tuple-element.50), channel_id=1, source_target_pairs={{0,8},{1,9},{2,10},{3,11},{4,12},{5,13},{6,14},{7,15},{8,0},{9,1},... | collective-permute-start | bytes 1572872 | tf_op jit(solution)/shard_map/ppermute | solution.py:13
  324.3 78.8 %collective-permute-start.7 = (f32[256,2,256]{2,1,0:T(2,128)S(1)}, f32[256,2,256]{2,1,0:T(2,128)S(1)}, u32[]{:S(2)}, u32[]{:S(2)}) collective-permute-start(f32[256,2,256]{2,1,0:T(2,128)S(1)} %get-tuple-element.51), channel_id=1, source_target_pairs={{0,4},{1,5},{2,6},{3,7},{4,0},{5,1},{6,2},{7,3},{8,12},{9,13},{10,... | collective-permute-start | bytes 1572872 | tf_op jit(solution)/shard_map/ppermute | solution.py:13
  331.3 72.2 %collective-permute-start.2 = (f32[256,2,256]{2,1,0:T(2,128)S(1)}, f32[256,2,256]{2,1,0:T(2,128)S(1)}, u32[]{:S(2)}, u32[]{:S(2)}) collective-permute-start(f32[256,2,256]{2,1,0:T(2,128)S(1)} %get-tuple-element.52), channel_id=1, source_target_pairs={{0,8},{1,9},{2,10},{3,11},{4,12},{5,13},{6,14},{7,15},{8,0},{9,1},... | collective-permute-start | bytes 1572872 | tf_op jit(solution)/shard_map/ppermute | solution.py:13
  338.3 76.0 %collective-permute-start.3 = (f32[256,2,256]{2,1,0:T(2,128)S(1)}, f32[256,2,256]{2,1,0:T(2,128)S(1)}, u32[]{:S(2)}, u32[]{:S(2)}) collective-permute-start(f32[256,2,256]{2,1,0:T(2,128)S(1)} %get-tuple-element.53), channel_id=1, source_target_pairs={{0,4},{1,5},{2,6},{3,7},{4,0},{5,1},{6,2},{7,3},{8,12},{9,13},{10,... | collective-permute-start | bytes 1572872 | tf_op jit(solution)/shard_map/ppermute | solution.py:13
Sparse Core Ops, SparseCore 0:
  11.1 85.1 all-gather.5
  99.3 77.2 all-gather.7
  302.2 168.3 all-reduce.11
  475.4 219.7 reduce-scatter.3
